TPU v7x, 768 devices: a whole 4x8x12 slice. The times are simulated.
768 devices in a mesh: grid: 96 (over z, x, core), slab: 8 (over y).
Axes of the slice: x: 4, y: 8, z: 12, core: 2. Of those that a mesh axis runs over, the one named last changes fastest.
Arguments:
- user_index: int32 [6291456], P(('grid', 'slab')), may hold values from 0 to 511
- item_index: int32 [6291456], P(('grid', 'slab')), may hold values from 0 to 3071
- week_index: int32 [6291456], P(('grid', 'slab')), may hold values from 0 to 511
- counts: bfloat16 [6291456], P(('grid', 'slab')), may hold values from 1 to 16
- item_factor: bfloat16 [24576, 128], P(('grid', 'slab')), may hold values from 0 to 4.053116e-05
- week_factor: bfloat16 [512, 128], P('slab'), may hold values from 0 to 0.001953125
Outputs:
- user_factor: float32 [49152, 128], P(('grid', 'slab'))
All inputs are finite; a program needn't handle non-finite values.
Results may differ from a plain program's by a relative error of at most 0.0043.
Values may be sent and summed in bfloat16 or wider, within the bound.
A program may use at most 32 MiB of HBM per device.

v0:
```python
import jax
import jax.numpy as jnp
from jax import lax
from jax.sharding import PartitionSpec as P

U_DEV = 64


block_rows = 256


def solve_rows(gram, rows):
    factor = jnp.linalg.cholesky(gram)
    middle = lax.linalg.triangular_solve(
        factor, rows, left_side=False, lower=True, transpose_a=True
    )
    return lax.linalg.triangular_solve(
        factor, middle, left_side=False, lower=True, transpose_a=False
    )


def local(user_index, item_index, week_index, counts, item_factor, week_factor):
    total_rows = user_index.shape[0]
    rank_width = item_factor.shape[1]
    u_blk = U_DEV * lax.axis_size("slab")
    steps_count = total_rows // block_rows
    week_all = lax.all_gather(week_factor, "slab", axis=0, tiled=True)
    week_gram = jnp.dot(week_all.T, week_all, preferred_element_type=jnp.float32)
    item_block = lax.all_gather(item_factor, "grid", axis=0, tiled=True)
    picked = item_block[item_index].astype(jnp.float32)
    week_columns = jnp.arange(week_all.shape[0], dtype=jnp.int32)

    def week_select(idx_block):
        onehot = (idx_block[:, None] == week_columns[None, :]).astype(jnp.bfloat16)
        return jnp.dot(onehot, week_all, preferred_element_type=jnp.float32)

    weekly = lax.map(week_select, week_index.reshape(steps_count, block_rows)).reshape(
        total_rows, rank_width
    )
    kr_rows = (counts.astype(jnp.float32)[:, None] * picked * weekly).astype(jnp.bfloat16)
    user_columns = jnp.arange(u_blk, dtype=jnp.int32)
    user_blocks = user_index.reshape(steps_count, block_rows)
    kr_blocks = kr_rows.reshape(steps_count, block_rows, rank_width)

    def accumulate(total, pair):
        idx_block, kr_block = pair
        onehot = (user_columns[:, None] == idx_block[None, :]).astype(jnp.bfloat16)
        return (total + jnp.dot(onehot, kr_block, preferred_element_type=jnp.float32), None)

    partial_rows, _ = lax.scan(
        accumulate, jnp.zeros((u_blk, rank_width), jnp.float32), (user_blocks, kr_blocks)
    )
    owned = lax.psum_scatter(partial_rows, "slab", scatter_dimension=0, tiled=True)
    local_gram = jnp.dot(item_factor.T, item_factor, preferred_element_type=jnp.float32)
    item_gram = lax.psum(local_gram, ("grid", "slab"))
    gram = item_gram * week_gram
    return solve_rows(gram, owned)


def solution(mesh):
    return jax.shard_map(
        local,
        mesh=mesh,
        in_specs=(
            P(("grid", "slab")),
            P(("grid", "slab")),
            P(("grid", "slab")),
            P(("grid", "slab")),
            P(("grid", "slab"), None),
            P("slab", None),
        ),
        out_specs=P(("grid", "slab"), None),
        check_vma=False,
    )
```

profile of v0, /device:TPU:1, one launch (start us, length us, event | category | flops | bytes accessed | tf_op | source)
XLA Modules:
  0.0 505.8 jit_solution(7299268306165964156)
XLA Ops:
  7.4 1.6 fusion.19
  9.1 86.6 %all_gather.6 = bf16[3072,128]{1,0:T(8,128)(2,1)S(1)} all-gather(bf16[32,128]{1,0:T(8,128)(2,1)} %param.14), channel_id=1, replica_groups=mesh['grid'=96,'slab'=8] {'grid'}, dimensions={0}, use_global_device_ids=true | all-gather | bytes 794624 | tf_op jit(solution)/shard_map/all_gather | solution.py:29
  95.6 21.2 %all_gather.7 = bf16[512,128]{1,0:T(8,128)(2,1)S(1)} all-gather(bf16[64,128]{1,0:T(8,128)(2,1)} %param.15), channel_id=1, replica_groups=mesh['grid'=96,'slab'=8] {'slab'}, dimensions={0}, use_global_device_ids=true | all-gather | bytes 147456 | tf_op jit(solution)/shard_map/all_gather | solution.py:27
  117.6 30.1 %while.22 = (s32[]{:T(128)}, f32[32,256,128]{2,1,0:T(8,128)}, s32[32,256]{1,0:T(8,128)S(1)}, bf16[512,128]{1,0:T(8,128)(2,1)S(1)}, s32[]{:T(128)}) while((s32[]{:T(128)}, f32[32,256,128]{2,1,0:T(8,128)}, s32[32,256]{1,0:T(8,128)S(1)}, bf16[512,128]{1,0:T(8,128)(2,1)S(1)}, s32[]{:T(128)}) %tuple.38), condition=%wide.region_1.2_spmd.clone, body=%wide.region_0.1_spmd.clone.sunk | while | flops 33685504 | bytes 265793 | solution.py:37
  119.6 0.9 fusion.31
  124.3 0.9 fusion.31
  131.8 0.9 fusion.31
  137.4 0.9 fusion.31
  146.8 0.9 fusion.31
  150.0 24.0 %gather_fusion = bf16[8192,128]{1,0:T(8,128)(2,1)S(1)} fusion(bf16[3072,128]{1,0:T(8,128)(2,1)S(1)} %all_gather.6, s32[8192]{0:T(1024)S(1)} %fusion.18), kind=kCustom, calls=%fused_computation | custom fusion | bytes 4227072 | tf_op jit(solution)/shard_map/gather | solution.py:30
  174.1 3.9 fusion.11
  177.9 36.4 %while.23 = (s32[]{:T(128)}, f32[512,128]{1,0:T(8,128)S(1)}, s32[32,256]{1,0:T(8,128)S(1)}, bf16[32,256,128]{2,1,0:T(8,128)(2,1)}, s32[]{:T(128)}, /*index=5*/s32[]{:T(128)}) while((s32[]{:T(128)}, f32[512,128]{1,0:T(8,128)S(1)}, s32[32,256]{1,0:T(8,128)S(1)}, bf16[32,256,128]{2,1,0:T(8,128)(2,1)}, s32[]{:T(128)}, ...), condition=%wide.region_3.4_spmd.clone, body=%wide.region_2.3_spmd.clone.sunk | while | flops 33816576 | bytes 593491 | solution.py:50
  177.9 1.1 convolution_add_fusion.2
  179.1 1.1 convolution_add_fusion.2
  180.2 1.1 convolution_add_fusion.2
  181.3 1.1 convolution_add_fusion.2
  182.5 1.1 convolution_add_fusion.2
  183.6 1.1 convolution_add_fusion.2
  184.8 1.1 convolution_add_fusion.2
  185.9 1.1 convolution_add_fusion.2
  187.0 1.1 convolution_add_fusion.2
  188.2 1.1 convolution_add_fusion.2
  189.3 1.1 convolution_add_fusion.2
  190.5 1.1 convolution_add_fusion.2
  191.6 1.1 convolution_add_fusion.2
  192.7 1.1 convolution_add_fusion.2
  193.9 1.1 convolution_add_fusion.2
  195.0 1.1 convolution_add_fusion.2
  196.2 1.1 convolution_add_fusion.2
  197.3 1.1 convolution_add_fusion.2
  198.4 1.1 convolution_add_fusion.2
  199.6 1.1 convolution_add_fusion.2
  200.7 1.1 convolution_add_fusion.2
  201.9 1.1 convolution_add_fusion.2
  203.0 1.1 convolution_add_fusion.2
  204.1 1.1 convolution_add_fusion.2
  205.3 1.1 convolution_add_fusion.2
  206.4 1.1 convolution_add_fusion.2
  207.6 1.1 convolution_add_fusion.2
  208.7 1.1 convolution_add_fusion.2
  209.8 1.1 convolution_add_fusion.2
  211.0 1.1 convolution_add_fusion.2
  212.1 1.1 convolution_add_fusion.2
  213.3 1.1 convolution_add_fusion.2
  215.1 257.4 %all-reduce.2.cloned.1.call-done = f32[128,128]{0,1:T(8,128)} async-done(((f32[128,128]{0,1:T(8,128)}), f32[128,128]{0,1:T(8,128)}) %all-reduce.2.cloned.1.call-update) | async-done | bytes 65552 | tf_op jit(solution)/shard_map/psum | solution.py:55
  472.4 1.1 convolution_multiply_fusion
  473.6 11.7 %cholesky.16 = f32[128,128]{1,0:T(8,128)S(1)} custom-call(f32[128,128]{1,0:T(8,128)S(1)} %fusion.17), custom_call_target="Cholesky" | custom-call | tf_op jit(solution)/shard_map/jit(cholesky)/cholesky | solution.py:13
  486.7 9.8 %custom-call.8 = f32[1,128,128]{1,2,0:T(8,128)S(1)} custom-call(f32[1,128,128]{2,1,0:T(8,128)S(1)} %fusion.12), custom_call_target="InvertDiagBlocksLowerTriangular" | custom-call | tf_op jit(solution)/shard_map/triangular_solve | solution.py:14
  (111 shorter events, 32.7 us)
Async XLA Ops:
  7.4 465.1 %all-reduce.2.cloned.1.call-start = ((), (), s32[]{:S(2)}) async-start(), calls=%async_computation.2 | async-start | bytes 131072 | tf_op jit(solution)/shard_map/psum | solution.py:55
  9.0 487.5 %reduce-scatter.2.cloned.1.call-start = ((), (), s32[]{:S(2)}) async-start(), calls=%async_computation.1 | async-start | bytes 294912 | tf_op jit(solution)/shard_map/reduce_scatter | solution.py:53
  214.4 0.7 copy-start
Sparse Core Ops, SparseCore 0:
  14.5 457.9 all-reduce.1
Sparse Core Ops, SparseCore 1:
  215.2 34.9 reduce-scatter.1
where the time goes:
time: 509 us; the launch traced here: 506 us
  waiting for transfers between devices  257 us (50%)
  blocking collectives  108 us (21%)
  matrix products  69.4 us (14%)
  local copies, waits for them, and re-layouts  27.6 us (5%)
  other arithmetic  27.5 us (5%)
  between operations  14.9 us (3%)
    psum x1, waiting for transfers between devices, local(): item_gram = lax.psum(local_gram, ('grid', 'slab'))  257 us
    all_gather x1, blocking collectives, local(): item_block = lax.all_gather(item_factor, 'grid', axis=0, tiled=True)  86.6 us
    dot_general x32, matrix products, accumulate(): jnp.dot(onehot, kr_block, preferred_element_type=jnp.float32)  35 us
    dot_general x32, matrix products, week_select(): return jnp.dot(onehot, week_all, preferred_element_type=jnp.float32)  29.9 us
    gather x1, local copies, waits for them, and re-layouts, local(): picked = item_block[item_index].astype(jnp.float32)  24 us
    all_gather x1, blocking collectives, local(): week_all = lax.all_gather(week_factor, 'slab', axis=0, tiled=True)  21.2 us
    another operation x3, other arithmetic, solve_rows(): factor = jnp.linalg.cholesky(gram)  12.4 us
    another operation x2, other arithmetic, solve_rows(): lax.linalg.triangular_solve(factor, rows, left_side=False, lower=True, tr...  10.5 us
  transfers between devices with their start and end apart: 2, of which 1 were waited for; matrix products, arithmetic and copies ran while one was open for 24% of the time, Pallas kernels for 0%

commit v1 on v0

v1 whole, which is shorter than its diff:
```python
import functools

import jax
import jax.numpy as jnp
from jax import lax
from jax.experimental import pallas as pl
from jax.experimental.pallas import tpu as pltpu
from jax.sharding import PartitionSpec as P

MESH = pl.DeviceIdType.MESH
N_X = 4
N_CORE = 2
HI = 4
WEEK_HI = 2
LANES = 128
N_BLK = 1024
PANEL = 32
F32 = jnp.float32
BF16 = jnp.bfloat16


def select_ones(row, table):
    h = table.shape[0]
    packed = jnp.broadcast_to(row, (16, LANES)).astype(jnp.int16)
    packed = jnp.concatenate([packed] * (h // 16), 0)
    return jnp.where(packed == table, BF16(1), BF16(0))


def dot_nt(a, b, **kw):
    return lax.dot_general(a, b, (((1,), (1,)), ((), ())), preferred_element_type=F32, **kw)


def dot_tn(a, b, **kw):
    return lax.dot_general(a, b, (((0,), (0,)), ((), ())), preferred_element_type=F32, **kw)


def invert_spd(a):
    n = a.shape[0]
    lane = lax.broadcasted_iota(jnp.int32, (PANEL, n), 1)
    sub = lax.broadcasted_iota(jnp.int32, (PANEL, n), 0)
    wide_lane = lax.broadcasted_iota(jnp.int32, (n, n), 1)

    def sweep(_, a):
        panel = a[:PANEL]
        x = panel
        for j in range(PANEL):
            at = lane == j
            col = jnp.broadcast_to(x[:, j : j + 1], (PANEL, n))
            inv = 1.0 / col[j : j + 1]
            row = jnp.where(at[:1], inv, x[j : j + 1] * inv)
            x = jnp.where(
                sub == j,
                jnp.broadcast_to(row, (PANEL, n)),
                jnp.where(at, 0.0, x) - col * row,
            )
        r = jnp.where(lane < PANEL, -x, x)
        rest = jnp.where(wide_lane < PANEL, 0.0, a) - dot_tn(panel, r, precision=lax.Precision.HIGHEST)
        a = jnp.concatenate([rest[PANEL:], r], 0)
        return pltpu.roll(a, n - PANEL, 1)

    return -lax.fori_loop(0, n // PANEL, sweep, a)


def kernel(
    n_z, n_y,
    user_ref, item_ix_ref, week_ix_ref, count_ref, item_ref, week_ref, out_ref,
    table, weeks, hot_item, hot_user, scaled, tt, wt, iota, hi, lo,
    total, gram_part, gram_in, gram_sum, gram_all, rows_in,
    z_send, z_recv, x_send, x_recv, c_send, c_recv, w_send, w_recv,
    g_send, g_recv, h_send, h_recv, m_send, m_recv,
):
    g = lax.axis_index("grid")
    s = lax.axis_index("slab")
    z = g // (N_X * N_CORE)
    x = (g // N_CORE) % N_X
    c = g % N_CORE
    rank = item_ref.shape[1]
    per = item_ref.shape[0]
    groups = user_ref.shape[0]
    n_all = groups * LANES
    users = hot_user.shape[0]
    n_lo = hot_item.shape[0]
    n_week = weeks.shape[0] * weeks.shape[1]

    def grid_id(zz, xx, cc):
        return (zz * N_X + xx) * N_CORE + cc

    def z_at(d):
        return lax.rem(z + d, n_z)

    def x_at(d):
        return lax.rem(x + d, N_X)

    def y_at(d):
        return lax.rem(s + d, n_y)

    z_peers = [(grid_id(z_at(d), x, c), s) for d in range(1, n_z)]
    x_peers = [(grid_id(z, x_at(d), c), s) for d in range(1, N_X)]
    c_peer = (grid_id(z, x, 1 - c), s)
    y_peers = [(g, y_at(d)) for d in range(1, n_y)]

    barrier = pltpu.get_barrier_semaphore()
    partners = z_peers + x_peers + [c_peer] + y_peers
    for who in partners:
        pl.semaphore_signal(barrier, inc=1, device_id=who, device_id_type=MESH)

    l = item_ix_ref[...]
    grid_of = lax.shift_right_logical(l, per.bit_length() - 1)
    l_z = lax.shift_right_logical(grid_of, 3)
    l_x = lax.shift_right_logical(grid_of, 1) & 3
    hi[...] = (grid_of & 1) * 2 + lax.shift_right_logical(l_x, 1)
    lo[...] = ((l_x & 1) * n_z + l_z) * per + (l & (per - 1))
    iota[...] = lax.broadcasted_iota(jnp.int32, iota.shape, 0).astype(jnp.int16)

    pl.semaphore_wait(barrier, len(partners))

    pending = []

    def send(src, dst, send_sem, recv_sem, who):
        copy = pltpu.make_async_remote_copy(
            src_ref=src, dst_ref=dst, send_sem=send_sem, recv_sem=recv_sem,
            device_id=who, device_id_type=MESH,
        )
        copy.start()
        pending.append(copy)

    def arrived(dst, send_sem, recv_sem, who):
        pltpu.make_async_remote_copy(
            src_ref=dst, dst_ref=dst, send_sem=send_sem, recv_sem=recv_sem,
            device_id=who, device_id_type=MESH,
        ).wait_recv()

    for d in range(1, n_z):
        send(item_ref, table.at[c, x, z], z_send.at[d - 1], z_recv.at[d - 1], z_peers[d - 1])
    for d in range(1, n_y):
        send(week_ref, weeks.at[s], w_send.at[d - 1], w_recv.at[d - 1], y_peers[d - 1])
    table[c, x, z] = item_ref[...]
    weeks[s] = week_ref[...]

    def make_user(r, carry):
        col = pl.ds(pl.multiple_of(r * LANES, LANES), LANES)
        hot_user[:, col] = select_ones(user_ref[pl.ds(r, 1), :], iota[:users])
        return carry

    lax.fori_loop(0, groups, make_user, 0)

    for d in range(1, n_z):
        arrived(table.at[c, x, z_at(n_z - d)], z_send.at[d - 1], z_recv.at[d - 1], z_peers[d - 1])
    for d in range(1, N_X):
        send(table.at[c, x], table.at[c, x], x_send.at[d - 1], x_recv.at[d - 1], x_peers[d - 1])
    send(table.at[c, x], table.at[c, x], c_send.at[0], c_recv.at[0], c_peer)

    def make_item(r, carry):
        col = pl.ds(pl.multiple_of(r * LANES, LANES), LANES)
        hot_item[:, col] = select_ones(lo[pl.ds(r, 1), :], iota[:n_lo])
        return carry

    lax.fori_loop(0, groups, make_item, 0)

    for d in range(1, N_X):
        spot = table.at[c, x_at(N_X - d)]
        arrived(spot, x_send.at[d - 1], x_recv.at[d - 1], x_peers[d - 1])
        send(spot, spot, c_send.at[d], c_recv.at[d], c_peer)

    eye = jnp.where(
        lax.broadcasted_iota(jnp.int32, (rank, rank), 0)
        == lax.broadcasted_iota(jnp.int32, (rank, rank), 1),
        1.0, 0.0,
    ).astype(BF16)

    for d in range(1, n_y):
        arrived(weeks.at[y_at(n_y - d)], w_send.at[d - 1], w_recv.at[d - 1], y_peers[d - 1])
    n_wlo = n_week // WEEK_HI
    for j in range(WEEK_HI):
        each = weeks.shape[0] // WEEK_HI
        part = weeks[j * each : (j + 1) * each].reshape(n_wlo, rank)
        wt[j * rank : (j + 1) * rank, :] = dot_nt(eye, part).astype(BF16)
    week_gram = dot_nt(wt[:rank], wt[:rank])
    for j in range(1, WEEK_HI):
        week_gram += dot_nt(wt[j * rank : (j + 1) * rank], wt[j * rank : (j + 1) * rank])

    per_blk = N_BLK // LANES

    def week_block(k, carry):
        hots = []
        for q in range(per_blk):
            w = week_ix_ref[pl.ds(k * per_blk + q, 1), :]
            hots.append(select_ones(w & (n_wlo - 1), iota[:n_wlo]))
        looked = jnp.dot(wt[...], jnp.concatenate(hots, 1), preferred_element_type=F32)
        for q in range(per_blk):
            w = week_ix_ref[pl.ds(k * per_blk + q, 1), :]
            top = jnp.broadcast_to(lax.shift_right_logical(w, n_wlo.bit_length() - 1), (rank, LANES))
            part = looked[:, q * LANES : (q + 1) * LANES]
            value = part[(WEEK_HI - 1) * rank :]
            for j in range(WEEK_HI - 2, -1, -1):
                value = jnp.where(top == j, part[j * rank : (j + 1) * rank], value)
            count = count_ref[pl.ds(k * per_blk + q, 1), :]
            col = pl.ds(pl.multiple_of(k * N_BLK + q * LANES, LANES), LANES)
            scaled[:, col] = value * count
        return carry

    lax.fori_loop(0, n_all // N_BLK, week_block, 0)

    for d in range(N_X):
        spot = table.at[1 - c, x_at((N_X - d) % N_X)]
        arrived(spot, c_send.at[d], c_recv.at[d], c_peer)

    half = N_X * N_CORE // HI
    item_gram = None
    for j in range(HI):
        first = (j * half) % N_X
        part = table[(j * half) // N_X, first : first + half].reshape(n_lo, rank)
        columns = dot_nt(eye, part).astype(BF16)
        tt[j * rank : (j + 1) * rank, :] = columns
        term = dot_nt(columns, columns)
        item_gram = term if item_gram is None else item_gram + term
    gram_part[...] = item_gram.reshape(gram_part.shape)
    for d in range(1, n_y):
        send(gram_part.at[y_at(d)], gram_in.at[d - 1], g_send.at[d - 1], g_recv.at[d - 1], y_peers[d - 1])

    total[...] = jnp.zeros_like(total)

    def main_block(k, carry):
        col = pl.ds(pl.multiple_of(k * N_BLK, N_BLK), N_BLK)
        looked = jnp.dot(tt[...], hot_item[:, col], preferred_element_type=F32)
        kr = []
        for q in range(per_blk):
            top = jnp.broadcast_to(hi[pl.ds(k * per_blk + q, 1), :], (rank, LANES))
            part = looked[:, q * LANES : (q + 1) * LANES]
            value = part[(HI - 1) * rank :]
            for j in range(HI - 2, -1, -1):
                value = jnp.where(top == j, part[j * rank : (j + 1) * rank], value)
            at = pl.ds(pl.multiple_of(k * N_BLK + q * LANES, LANES), LANES)
            kr.append((value * scaled[:, at]).astype(BF16))
        add = dot_nt(hot_user[:, col], jnp.concatenate(kr, 1))
        total[...] += add.reshape(total.shape)
        return carry

    blocks = n_all // N_BLK
    lax.fori_loop(0, blocks // 2, main_block, 0)

    for d in range(1, n_y):
        arrived(gram_in.at[d - 1], g_send.at[d - 1], g_recv.at[d - 1], y_peers[d - 1])
    piece = gram_part[s]
    for d in range(1, n_y):
        piece = piece + gram_in[d - 1]
    gram_sum[...] = piece
    gram_all[s] = piece
    for d in range(1, n_y):
        send(gram_sum, gram_all.at[s], h_send.at[d - 1], h_recv.at[d - 1], y_peers[d - 1])

    lax.fori_loop(blocks // 2, blocks, main_block, 0)

    for d in range(1, n_y):
        send(total.at[y_at(d)], rows_in.at[d - 1], m_send.at[d - 1], m_recv.at[d - 1], y_peers[d - 1])

    for d in range(1, n_y):
        arrived(gram_all.at[y_at(n_y - d)], h_send.at[d - 1], h_recv.at[d - 1], y_peers[d - 1])
    inverse = invert_spd(gram_all[...].reshape(rank, rank) * week_gram)

    for d in range(1, n_y):
        arrived(rows_in.at[d - 1], m_send.at[d - 1], m_recv.at[d - 1], y_peers[d - 1])
    rows = total[s]
    for d in range(1, n_y):
        rows = rows + rows_in[d - 1]
    out_ref[...] = jnp.dot(rows, inverse, preferred_element_type=F32, precision=lax.Precision.HIGHEST)

    for copy in pending:
        copy.wait_send()


def local(n_grid, n_y, user_index, item_index, week_index, counts, item_factor, week_factor):
    n_all = user_index.shape[0]
    groups = n_all // LANES
    per, rank = item_factor.shape
    n_z = n_grid // (N_X * N_CORE)
    n_item = per * n_grid
    n_lo = n_item // HI
    n_week = week_factor.shape[0] * n_y
    u_dev = 64
    users = u_dev * n_y
    dma = pltpu.SemaphoreType.DMA
    return pl.pallas_call(
        functools.partial(kernel, n_z, n_y),
        out_shape=jax.ShapeDtypeStruct((u_dev, rank), F32),
        in_specs=[pl.BlockSpec(memory_space=pltpu.VMEM)] * 6,
        out_specs=pl.BlockSpec(memory_space=pltpu.VMEM),
        scratch_shapes=[
            pltpu.VMEM((N_CORE, N_X, n_z, per, rank), BF16),
            pltpu.VMEM((n_y,) + week_factor.shape, BF16),
            pltpu.VMEM((n_lo, n_all), BF16),
            pltpu.VMEM((users, n_all), BF16),
            pltpu.VMEM((rank, n_all), F32),
            pltpu.VMEM((HI * rank, n_lo), BF16),
            pltpu.VMEM((WEEK_HI * rank, n_week // WEEK_HI), BF16),
            pltpu.VMEM((max(n_lo, users), LANES), jnp.int16),
            pltpu.VMEM((groups, LANES), jnp.int32),
            pltpu.VMEM((groups, LANES), jnp.int32),
            pltpu.VMEM((n_y, u_dev, rank), F32),
            pltpu.VMEM((n_y, rank // n_y, rank), F32),
            pltpu.VMEM((n_y - 1, rank // n_y, rank), F32),
            pltpu.VMEM((rank // n_y, rank), F32),
            pltpu.VMEM((n_y, rank // n_y, rank), F32),
            pltpu.VMEM((n_y - 1, u_dev, rank), F32),
        ]
        + [dma((n_z - 1,))] * 2
        + [dma((N_X - 1,))] * 2
        + [dma((N_X,))] * 2
        + [dma((n_y - 1,))] * 8,
        compiler_params=pltpu.CompilerParams(
            collective_id=0, has_side_effects=True, vmem_limit_bytes=48 * 2**20
        ),
        name="mttkrp_solve",
    )(
        user_index.reshape(groups, LANES),
        item_index.reshape(groups, LANES),
        week_index.reshape(groups, LANES),
        counts.astype(F32).reshape(groups, LANES),
        item_factor,
        week_factor,
    )


def solution(mesh):
    return jax.shard_map(
        functools.partial(local, mesh.shape["grid"], mesh.shape["slab"]),
        mesh=mesh,
        in_specs=(
            P(("grid", "slab")),
            P(("grid", "slab")),
            P(("grid", "slab")),
            P(("grid", "slab")),
            P(("grid", "slab"), None),
            P("slab", None),
        ),
        out_specs=P(("grid", "slab"), None),
        check_vma=False,
    )
```

time: 509 us -> 61.9 us (0.12)
  waiting for transfers between devices: 257 us -> 0 us
  blocking collectives: 108 us -> 0 us
  matrix products: 69.4 us -> 0 us
  Pallas kernels: 0 us -> 57.8 us
  other arithmetic: 27.5 us -> 0.73 us
  local copies, waits for them, and re-layouts: 27.6 us -> 2.88 us
  between operations: 14.9 us -> 0.01 us
    psum x1 -> x0, waiting for transfers between devices: 257 us -> none  [local(): item_gram = lax.psum(local_gram, ('grid', 'slab'))]
    all_gather x2 -> x0, blocking collectives: 108 us -> none  [the longest x1 86.6 us: local(): item_block = lax.all_gather(item_factor, 'grid', axis=0, tiled=True)]
    dot_general x66 -> x0, matrix products: 67.6 us -> none  [the longest x32 35 us: accumulate(): jnp.dot(onehot, kr_block, preferred_element_type=jnp.float32)]
    pallas_call x0 -> x1, Pallas kernels: none -> 57.8 us  [local(): pl.pallas_call(functools.partial(kernel, n_z, n_y), out_shape=jax.ShapeDt...]
    gather x1 -> x0, local copies, waits for them, and re-layouts: 24 us -> none  [local(): picked = item_block[item_index].astype(jnp.float32)]
    another operation x5 -> x0, other arithmetic: 22.9 us -> none  [the longest x3 12.4 us: solve_rows(): factor = jnp.linalg.cholesky(gram)]
  transfers between devices with their start and end apart: 2 -> 0, of which waited for: 1 -> 0; matrix products, arithmetic and copies ran while one was open for 24% -> 0% of each run, Pallas kernels for 0% -> 0%
where the time goes in v1:
time: 61.9 us; the launch traced here: 61.4 us
  Pallas kernels  57.8 us (93%)
  local copies, waits for them, and re-layouts  2.88 us (5%)
  other arithmetic  0.73 us (1%)
    pallas_call x1, Pallas kernels, local(): pl.pallas_call(functools.partial(kernel, n_z, n_y), out_shape=jax.ShapeDt...  57.8 us
    unnamed x11, local copies, waits for them, and re-layouts  2.88 us

profile of v1, /device:TPU:1, one launch (start us, length us, event | category | flops | bytes accessed | tf_op | source)
XLA Modules:
  0.0 61.4 jit_solution(13594768723508225790)
XLA Ops:
  0.0 0.0 copy-start
  0.0 0.0 copy-start.3
  0.0 0.7 %bitcast_convert_fusion.count_ref = f32[64,128]{1,0:T(8,128)S(1)} fusion(bf16[8192]{0:T(1024)(128)(2,1)} %param.9), kind=kLoop, calls=%fused_computation | loop fusion | flops 8192 | bytes 49152 | tf_op jit(solution)/shard_map/reshape | solution.py:318
  0.7 0.0 copy-done
  0.8 0.0 copy-done.3
  0.8 0.0 copy-start.1
  0.8 0.8 %copy-done.1 = s32[8192]{0:T(1024)S(1)} copy-done((s32[8192]{0:T(1024)S(1)}, s32[8192]{0:T(1024)}, u32[]{:S(2)}) %copy-start.1) | copy-done | bytes 32792
  1.5 0.0 copy-start.2
  1.5 0.8 %copy-done.2 = s32[8192]{0:T(1024)S(1)} copy-done((s32[8192]{0:T(1024)S(1)}, s32[8192]{0:T(1024)}, u32[]{:S(2)}) %copy-start.2) | copy-done | bytes 32792
  2.3 0.0 copy-start.4
  2.3 0.7 %copy-done.4 = bf16[32,128]{1,0:T(8,128)(2,1)S(1)} copy-done((bf16[32,128]{1,0:T(8,128)(2,1)S(1)}, bf16[32,128]{1,0:T(8,128)(2,1)}, u32[]{:S(2)}) %copy-start.4) | copy-done | bytes 8216
  3.0 57.8 %mttkrp_solve.1 = f32[64,128]{1,0:T(8,128)S(1)} custom-call(s32[64,128]{1,0:T(8,128)S(1)} %bitcast.6, s32[64,128]{1,0:T(8,128)S(1)} %bitcast.7, s32[64,128]{1,0:T(8,128)S(1)} %bitcast.8, f32[64,128]{1,0:T(8,128)S(1)} %bitcast_convert_fusion.count_ref, bf16[32,128]{1,0:T(8,128)(2,1)S(1)} %copy-done.4, bf16[64,128]{1,0:T(8,128)(2,1)S(1)} %copy-done.3), custom_call_target="tpu_custom_call" | custom-call | tf_op jit(solution)/shard_map/mttkrp_solve/pallas_call | solution.py:283
  60.8 0.6 %copy.8 = f32[64,128]{1,0:T(8,128)} copy(f32[64,128]{1,0:T(8,128)S(1)} %mttkrp_solve.1) | data formatting | bytes 65536
Async XLA Ops:
  0.0 0.8 %copy-start = (s32[8192]{0:T(1024)S(1)}, s32[8192]{0:T(1024)}, u32[]{:S(2)}) copy-start(s32[8192]{0:T(1024)} %param.6) | copy-start | bytes 98308
  0.0 0.8 %copy-start.3 = (bf16[64,128]{1,0:T(8,128)(2,1)S(1)}, bf16[64,128]{1,0:T(8,128)(2,1)}, u32[]{:S(2)}) copy-start(bf16[64,128]{1,0:T(8,128)(2,1)} %week_ref.1) | copy-start | bytes 49156
  0.8 0.8 %copy-start.1 = (s32[8192]{0:T(1024)S(1)}, s32[8192]{0:T(1024)}, u32[]{:S(2)}) copy-start(s32[8192]{0:T(1024)} %param.7) | copy-start | bytes 98308
  1.5 0.8 %copy-start.2 = (s32[8192]{0:T(1024)S(1)}, s32[8192]{0:T(1024)}, u32[]{:S(2)}) copy-start(s32[8192]{0:T(1024)} %param.8) | copy-start | bytes 98308
  2.3 0.7 %copy-start.4 = (bf16[32,128]{1,0:T(8,128)(2,1)S(1)}, bf16[32,128]{1,0:T(8,128)(2,1)}, u32[]{:S(2)}) copy-start(bf16[32,128]{1,0:T(8,128)(2,1)} %item_ref.1) | copy-start | bytes 24580

commit v2 on v1

v2 whole, which is shorter than its diff:
```python
import functools

import jax
import jax.numpy as jnp
from jax import lax
from jax.experimental import pallas as pl
from jax.experimental.pallas import tpu as pltpu
from jax.sharding import PartitionSpec as P

MESH = pl.DeviceIdType.MESH
N_X = 4
N_CORE = 2
HI = 4
WEEK_HI = 2
LANES = 128
N_BLK = 2048
WEEK_BLK = 1024
PIVOTS = 4
PANEL = 32
F32 = jnp.float32
BF16 = jnp.bfloat16


def select_ones(row, table):
    h = table.shape[0]
    packed = jnp.broadcast_to(row, (16, LANES)).astype(jnp.int16)
    packed = jnp.concatenate([packed] * (h // 16), 0)
    return jnp.where(packed == table, BF16(1), BF16(0))


def dot_nt(a, b, **kw):
    return lax.dot_general(a, b, (((1,), (1,)), ((), ())), preferred_element_type=F32, **kw)


def dot_tn(a, b, **kw):
    return lax.dot_general(a, b, (((0,), (0,)), ((), ())), preferred_element_type=F32, **kw)


def invert_spd(a):
    n = a.shape[0]
    lane = lax.broadcasted_iota(jnp.int32, (PANEL, n), 1)
    sub = lax.broadcasted_iota(jnp.int32, (PANEL, n), 0)
    wide_lane = lax.broadcasted_iota(jnp.int32, (n, n), 1)
    m = PIVOTS

    def sweep(_, a):
        panel = a[:PANEL]
        x = panel
        for j in range(0, PANEL, m):
            cols = [jnp.broadcast_to(x[:, j + t : j + t + 1], (PANEL, n)) for t in range(m)]
            w = [[cols[t][j + r : j + r + 1] for t in range(m)] for r in range(m)]
            for p in range(m):
                inv = 1.0 / w[p][p]
                w[p] = [inv if t == p else w[p][t] * inv for t in range(m)]
                for r in range(m):
                    if r != p:
                        f = w[r][p]
                        w[r] = [-f * inv if t == p else w[r][t] - f * w[p][t] for t in range(m)]
            rows = []
            for r in range(m):
                row = w[r][0] * x[j : j + 1]
                for t in range(1, m):
                    row = row + w[r][t] * x[j + t : j + t + 1]
                for t in range(m):
                    row = jnp.where(lane[:1] == j + t, w[r][t], row)
                rows.append(row)
            x = jnp.where((lane >= j) & (lane < j + m), 0.0, x)
            for t in range(m):
                x = x - cols[t] * rows[t]
            for t in range(m):
                x = jnp.where(sub == j + t, jnp.broadcast_to(rows[t], (PANEL, n)), x)
        r = jnp.where(lane < PANEL, -x, x)
        rest = jnp.where(wide_lane < PANEL, 0.0, a) - dot_tn(panel, r, precision=lax.Precision.HIGHEST)
        a = jnp.concatenate([rest[PANEL:], r], 0)
        return pltpu.roll(a, n - PANEL, 1)

    return -lax.fori_loop(0, n // PANEL, sweep, a)


def kernel(
    n_z, n_y,
    user_hbm, item_ix_hbm, week_ix_hbm, count_hbm, item_hbm, week_hbm, out_ref,
    user_ref, item_ix_ref, week_ix_ref, count_in, item_ref, week_ref, count_ref,
    table, weeks, hot_item, hot_user, scaled, kr_all, tt, wt, iota, hi, lo,
    total, gram_part, gram_in, gram_all, rows_in,
    in_sem, z_send, z_recv, x_send, x_recv, c_send, c_recv, w_send, w_recv,
    g_send, g_recv, h_send, h_recv, m_send, m_recv,
):
    loads = []
    for k, (src, dst) in enumerate([
        (item_hbm, item_ref), (week_hbm, week_ref), (user_hbm, user_ref),
        (item_ix_hbm, item_ix_ref), (week_ix_hbm, week_ix_ref), (count_hbm, count_in),
    ]):
        copy = pltpu.make_async_copy(src, dst, in_sem.at[k])
        copy.start()
        loads.append(copy)
    g = lax.axis_index("grid")
    s = lax.axis_index("slab")
    z = g // (N_X * N_CORE)
    x = (g // N_CORE) % N_X
    c = g % N_CORE
    rank = item_ref.shape[1]
    per = item_ref.shape[0]
    groups = user_ref.shape[0]
    n_all = groups * LANES
    users = hot_user.shape[0]
    n_lo = hot_item.shape[0]
    n_week = weeks.shape[0] * weeks.shape[1]
    u_dev = out_ref.shape[0]

    def grid_id(zz, xx, cc):
        return (zz * N_X + xx) * N_CORE + cc

    def z_at(d):
        return lax.rem(z + d, n_z)

    def x_at(d):
        return lax.rem(x + d, N_X)

    def y_at(d):
        return lax.rem(s + d, n_y)

    z_peers = [(grid_id(z_at(d), x, c), s) for d in range(1, n_z)]
    x_peers = [(grid_id(z, x_at(d), c), s) for d in range(1, N_X)]
    c_peer = (grid_id(z, x, 1 - c), s)
    y_peers = [(g, y_at(d)) for d in range(1, n_y)]
    around = [(dx, dc) for dx in range(N_X) for dc in range(N_CORE) if dx or dc]

    def core_at(dc):
        return 1 - c if dc else c

    around_peers = [(grid_id(z, x_at(dx), core_at(dc)), s) for dx, dc in around]

    barrier = pltpu.get_barrier_semaphore()
    partners = around_peers + z_peers + y_peers
    for who in partners:
        pl.semaphore_signal(barrier, inc=1, device_id=who, device_id_type=MESH)

    iota[...] = lax.broadcasted_iota(jnp.int32, iota.shape, 0).astype(jnp.int16)
    for copy in loads:
        copy.wait()

    mid = n_z // 2
    l = item_ix_ref[...]
    grid_of = lax.shift_right_logical(l, per.bit_length() - 1)
    l_z = lax.shift_right_logical(grid_of, 3)
    l_x = lax.shift_right_logical(grid_of, 1) & 3
    hi[...] = (grid_of & 1) * 2 + lax.shift_right_logical(l_x, 1)
    l_slot = l_z + (mid - z)
    l_slot = jnp.where(l_slot < 0, l_slot + n_z, jnp.where(l_slot >= n_z, l_slot - n_z, l_slot))
    lo[...] = ((l_x & 1) * n_z + l_slot) * per + (l & (per - 1))
    user_ref[...] = (user_ref[...] + (n_y - lax.rem(s + 2, n_y)) * u_dev) & (users - 1)
    count_ref[...] = count_in[...].astype(F32)

    pl.semaphore_wait(barrier, len(partners))

    pending = []

    def send(src, dst, send_sem, recv_sem, who):
        copy = pltpu.make_async_remote_copy(
            src_ref=src, dst_ref=dst, send_sem=send_sem, recv_sem=recv_sem,
            device_id=who, device_id_type=MESH,
        )
        copy.start()
        pending.append(copy)

    def arrived(dst, send_sem, recv_sem, who):
        pltpu.make_async_remote_copy(
            src_ref=dst, dst_ref=dst, send_sem=send_sem, recv_sem=recv_sem,
            device_id=who, device_id_type=MESH,
        ).wait_recv()

    by_reach = sorted(range(1, n_z), key=lambda d: -min(d, n_z - d))
    for d in by_reach:
        send(item_ref, table.at[c, x, (mid - d) % n_z], z_send.at[d - 1], z_recv.at[d - 1], z_peers[d - 1])
    table[c, x, mid] = item_ref[...]
    far_y = sorted(range(1, n_y), key=lambda d: -min(d, n_y - d))
    for d in far_y:
        send(week_ref, weeks.at[s], w_send.at[d - 1], w_recv.at[d - 1], y_peers[d - 1])
    weeks[s] = week_ref[...]

    def make_user(r, carry):
        col = pl.ds(pl.multiple_of(r * LANES, LANES), LANES)
        hot_user[:, col] = select_ones(user_ref[pl.ds(r, 1), :], iota[:users])
        return carry

    def make_item(r, carry):
        col = pl.ds(pl.multiple_of(r * LANES, LANES), LANES)
        hot_item[:, col] = select_ones(lo[pl.ds(r, 1), :], iota[:n_lo])
        return carry

    far_x = sorted(range(1, N_X), key=lambda d: -min(d, N_X - d))

    def z_arrive(lo_reach, hi_reach):
        for reach in range(lo_reach, hi_reach + 1):
            for d in sorted({reach, n_z - reach}):
                arrived(table.at[c, x, (mid - d) % n_z], z_send.at[d - 1], z_recv.at[d - 1], z_peers[d - 1])

    def pass_on(first, count):
        part = table.at[c, x, pl.ds(first, count)]
        for d in far_x:
            copy = pltpu.make_async_remote_copy(
                src_ref=part, dst_ref=part, send_sem=x_send.at[d - 1], recv_sem=x_recv.at[d - 1],
                device_id=x_peers[d - 1], device_id_type=MESH,
            )
            copy.start()

    lax.fori_loop(0, groups, make_user, 0)
    near = min(2, mid - 1)
    wide = max(near, mid - 2)
    z_arrive(1, near)
    pass_on(mid - near, 2 * near + 1)
    lax.fori_loop(0, groups // 2, make_item, 0)
    if wide > near:
        z_arrive(near + 1, wide)
        pass_on(mid - wide, wide - near)
        pass_on(mid + near + 1, wide - near)
    lax.fori_loop(groups // 2, groups, make_item, 0)
    z_arrive(wide + 1, mid)
    pass_on(0, mid - wide)
    if n_z - (mid + wide + 1):
        pass_on(mid + wide + 1, n_z - (mid + wide + 1))
    send(table.at[c, x], table.at[c, x], c_send.at[0], c_recv.at[0], c_peer)

    eye = jnp.where(
        lax.broadcasted_iota(jnp.int32, (rank, rank), 0)
        == lax.broadcasted_iota(jnp.int32, (rank, rank), 1),
        1.0, 0.0,
    ).astype(BF16)

    for d in range(1, n_y):
        arrived(weeks.at[y_at(n_y - d)], w_send.at[d - 1], w_recv.at[d - 1], y_peers[d - 1])
    n_wlo = n_week // WEEK_HI
    for j in range(WEEK_HI):
        each = weeks.shape[0] // WEEK_HI
        part = weeks[j * each : (j + 1) * each].reshape(n_wlo, rank)
        wt[j * rank : (j + 1) * rank, :] = dot_nt(eye, part).astype(BF16)
    week_gram = dot_nt(wt[:rank], wt[:rank])
    for j in range(1, WEEK_HI):
        week_gram += dot_nt(wt[j * rank : (j + 1) * rank], wt[j * rank : (j + 1) * rank])

    per_week = WEEK_BLK // LANES

    def week_block(k, carry):
        hots = []
        for q in range(per_week):
            w = week_ix_ref[pl.ds(k * per_week + q, 1), :]
            hots.append(select_ones(w & (n_wlo - 1), iota[:n_wlo]))
        looked = jnp.dot(wt[...], jnp.concatenate(hots, 1), preferred_element_type=F32)
        for q in range(per_week):
            w = week_ix_ref[pl.ds(k * per_week + q, 1), :]
            top = jnp.broadcast_to(lax.shift_right_logical(w, n_wlo.bit_length() - 1), (rank, LANES))
            part = looked[:, q * LANES : (q + 1) * LANES]
            value = part[(WEEK_HI - 1) * rank :]
            for j in range(WEEK_HI - 2, -1, -1):
                value = jnp.where(top == j, part[j * rank : (j + 1) * rank], value)
            count = count_ref[pl.ds(k * per_week + q, 1), :]
            col = pl.ds(pl.multiple_of(k * WEEK_BLK + q * LANES, LANES), LANES)
            scaled[:, col] = value * count
        return carry

    lax.fori_loop(0, n_all // WEEK_BLK, week_block, 0)

    for d in range(1, N_X):
        spot = table.at[c, x_at(N_X - d)]
        arrived(spot, x_send.at[d - 1], x_recv.at[d - 1], x_peers[d - 1])
        send(spot, spot, c_send.at[d], c_recv.at[d], c_peer)

    half = N_X * N_CORE // HI

    def turn(core):
        sums = None
        for j in range(HI // N_CORE):
            part = table[core, j * half : (j + 1) * half].reshape(n_lo, rank)
            columns = dot_nt(eye, part).astype(BF16)
            tt[pl.ds(pl.multiple_of((core * (HI // N_CORE) + j) * rank, rank), rank), :] = columns
            term = dot_nt(columns, columns)
            sums = term if sums is None else sums + term
        return sums

    item_gram = turn(c)
    for d in range(N_X):
        spot = table.at[1 - c, x_at((N_X - d) % N_X)]
        arrived(spot, c_send.at[d], c_recv.at[d], c_peer)
    item_gram = item_gram + turn(1 - c)
    gram_part[...] = item_gram.reshape(gram_part.shape)
    e = x * N_CORE + c
    for d in far_y:
        send(gram_part.at[e], gram_in.at[d - 1], g_send.at[d - 1], g_recv.at[d - 1], y_peers[d - 1])

    per_blk = N_BLK // LANES

    def main_block(k, carry):
        col = pl.ds(pl.multiple_of(k * N_BLK, N_BLK), N_BLK)
        looked = jnp.dot(tt[...], hot_item[:, col], preferred_element_type=F32)
        kr = []
        for q in range(per_blk):
            top = jnp.broadcast_to(hi[pl.ds(k * per_blk + q, 1), :], (rank, LANES))
            part = looked[:, q * LANES : (q + 1) * LANES]
            value = part[(HI - 1) * rank :]
            for j in range(HI - 2, -1, -1):
                value = jnp.where(top == j, part[j * rank : (j + 1) * rank], value)
            at = pl.ds(pl.multiple_of(k * N_BLK + q * LANES, LANES), LANES)
            kr.append((value * scaled[:, at]).astype(BF16))
        kr_all[:, col] = jnp.concatenate(kr, 1)
        return carry

    blocks = n_all // N_BLK
    first = 3 * blocks // 4
    lax.fori_loop(0, first, main_block, 0)

    for d in range(1, n_y):
        arrived(gram_in.at[d - 1], g_send.at[d - 1], g_recv.at[d - 1], y_peers[d - 1])
    piece = gram_part[e]
    for d in range(1, n_y):
        piece = piece + gram_in[d - 1]
    gram_all[e] = piece
    for k in range(len(around)):
        send(gram_all.at[e], gram_all.at[e], h_send.at[k], h_recv.at[k], around_peers[k])

    lax.fori_loop(first, blocks, main_block, 0)

    half_users = users // 2
    for side in range(2):
        span = slice(side * half_users, (side + 1) * half_users)
        sums = dot_nt(hot_user[span, :], kr_all[...])
        mine = range(side * n_y // 2, (side + 1) * n_y // 2)
        total[side * n_y // 2 : (side + 1) * n_y // 2] = sums.reshape(n_y // 2, u_dev, rank)
        for d in far_y:
            if (d - 2) % n_y in mine:
                send(total.at[(d - 2) % n_y], rows_in.at[d - 1], m_send.at[d - 1], m_recv.at[d - 1], y_peers[d - 1])

    for k, (dx, dc) in enumerate(around):
        spot = gram_all.at[x_at((N_X - dx) % N_X) * N_CORE + core_at(dc)]
        arrived(spot, h_send.at[k], h_recv.at[k], around_peers[k])
    inverse = invert_spd(gram_all[...].reshape(rank, rank) * week_gram)

    for d in range(1, n_y):
        arrived(rows_in.at[d - 1], m_send.at[d - 1], m_recv.at[d - 1], y_peers[d - 1])
    rows = total[(0 - 2) % n_y]
    for d in range(1, n_y):
        rows = rows + rows_in[d - 1]
    out_ref[...] = jnp.dot(rows, inverse, preferred_element_type=F32, precision=lax.Precision.HIGHEST)

    for copy in pending:
        copy.wait_send()
    for d in range(1, N_X):
        slab = table.at[c, x]
        pltpu.make_async_remote_copy(
            src_ref=slab, dst_ref=slab, send_sem=x_send.at[d - 1], recv_sem=x_recv.at[d - 1],
            device_id=x_peers[d - 1], device_id_type=MESH,
        ).wait_send()


def local(n_grid, n_y, user_index, item_index, week_index, counts, item_factor, week_factor):
    n_all = user_index.shape[0]
    groups = n_all // LANES
    per, rank = item_factor.shape
    n_z = n_grid // (N_X * N_CORE)
    n_item = per * n_grid
    n_lo = n_item // HI
    n_week = week_factor.shape[0] * n_y
    u_dev = 64
    users = u_dev * n_y
    dma = pltpu.SemaphoreType.DMA
    return pl.pallas_call(
        functools.partial(kernel, n_z, n_y),
        out_shape=jax.ShapeDtypeStruct((u_dev, rank), F32),
        in_specs=[pl.BlockSpec(memory_space=pltpu.MemorySpace.HBM)] * 6,
        out_specs=pl.BlockSpec(memory_space=pltpu.VMEM),
        scratch_shapes=[
            pltpu.VMEM((groups, LANES), jnp.int32),
            pltpu.VMEM((groups, LANES), jnp.int32),
            pltpu.VMEM((groups, LANES), jnp.int32),
            pltpu.VMEM((groups, LANES), BF16),
            pltpu.VMEM(item_factor.shape, BF16),
            pltpu.VMEM(week_factor.shape, BF16),
            pltpu.VMEM((groups, LANES), F32),
            pltpu.VMEM((N_CORE, N_X, n_z, per, rank), BF16),
            pltpu.VMEM((n_y,) + week_factor.shape, BF16),
            pltpu.VMEM((n_lo, n_all), BF16),
            pltpu.VMEM((users, n_all), BF16),
            pltpu.VMEM((rank, n_all), F32),
            pltpu.VMEM((rank, n_all), BF16),
            pltpu.VMEM((HI * rank, n_lo), BF16),
            pltpu.VMEM((WEEK_HI * rank, n_week // WEEK_HI), BF16),
            pltpu.VMEM((max(n_lo, users), LANES), jnp.int16),
            pltpu.VMEM((groups, LANES), jnp.int32),
            pltpu.VMEM((groups, LANES), jnp.int32),
            pltpu.VMEM((n_y, u_dev, rank), F32),
            pltpu.VMEM((n_y, rank // n_y, rank), F32),
            pltpu.VMEM((n_y - 1, rank // n_y, rank), F32),
            pltpu.VMEM((n_y, rank // n_y, rank), F32),
            pltpu.VMEM((n_y - 1, u_dev, rank), F32),
        ]
        + [dma((6,))]
        + [dma((n_z - 1,))] * 2
        + [dma((N_X - 1,))] * 2
        + [dma((N_X,))] * 2
        + [dma((n_y - 1,))] * 8,
        compiler_params=pltpu.CompilerParams(
            collective_id=0, has_side_effects=True, vmem_limit_bytes=62914560
        ),
        name="mttkrp_solve",
    )(
        user_index.reshape(groups, LANES),
        item_index.reshape(groups, LANES),
        week_index.reshape(groups, LANES),
        counts.reshape(groups, LANES),
        item_factor,
        week_factor,
    )


def solution(mesh):
    return jax.shard_map(
        functools.partial(local, mesh.shape["grid"], mesh.shape["slab"]),
        mesh=mesh,
        in_specs=(
            P(("grid", "slab")),
            P(("grid", "slab")),
            P(("grid", "slab")),
            P(("grid", "slab")),
            P(("grid", "slab"), None),
            P("slab", None),
        ),
        out_specs=P(("grid", "slab"), None),
        check_vma=False,
    )
```

time: 61.9 us -> 56.4 us (0.911)
  Pallas kernels: 57.8 us -> 54.7 us
  local copies, waits for them, and re-layouts: 2.88 us -> 1.38 us
  other arithmetic: 0.73 us -> 0 us
    pallas_call x1, Pallas kernels: 57.8 us -> 54.7 us  [local(): pl.pallas_call(functools.partial(kernel, n_z, n_y), out_shape=jax.ShapeDt...]
    unnamed x11 -> x1, local copies, waits for them, and re-layouts: 2.88 us -> 1.38 us
    reshape x1 -> x0, other arithmetic: 0.73 us -> none  [local(): counts.astype(F32).reshape(groups, LANES)]
where the time goes in v2:
time: 56.4 us; the launch traced here: 56.1 us
  Pallas kernels  54.7 us (97%)
  local copies, waits for them, and re-layouts  1.38 us (2%)
    pallas_call x1, Pallas kernels, local(): pl.pallas_call(functools.partial(kernel, n_z, n_y), out_shape=jax.ShapeDt...  54.7 us
    unnamed x1, local copies, waits for them, and re-layouts  1.38 us

profile of v2, /device:TPU:1, one launch (start us, length us, event | category | flops | bytes accessed | tf_op | source)
XLA Modules:
  0.0 56.1 jit_solution(2504466612953586089)
XLA Ops:
  0.0 54.7 %mttkrp_solve.1 = f32[64,128]{1,0:T(8,128)} custom-call(s32[64,128]{1,0:T(8,128)} %bitcast.4, s32[64,128]{1,0:T(8,128)} %bitcast.5, s32[64,128]{1,0:T(8,128)} %bitcast.6, bf16[64,128]{1,0:T(8,128)(2,1)} %bitcast.7, bf16[32,128]{1,0:T(8,128)(2,1)} %item_hbm.1, bf16[64,128]{1,0:T(8,128)(2,1)} %week_hbm.1), custom_call_target="tpu_custom_call" | custom-call | tf_op jit(solution)/shard_map/mttkrp_solve/pallas_call | solution.py:366
  54.7 1.4 %copy.8 = f32[64,128]{1,0:T(8,128)} copy(f32[64,128]{1,0:T(8,128)} %mttkrp_solve.1) | data formatting | bytes 65536

commit v3 on v2

--- a/solution.py
+++ b/solution.py
@@ -132,28 +132,17 @@
     around_peers = [(grid_id(z, x_at(dx), core_at(dc)), s) for dx, dc in around]
 
     barrier = pltpu.get_barrier_semaphore()
-    partners = around_peers + z_peers + y_peers
+    by_reach = sorted(range(1, n_z), key=lambda d: -min(d, n_z - d))
+    far_y = sorted(range(1, n_y), key=lambda d: -min(d, n_y - d))
+    partners = [z_peers[d - 1] for d in by_reach] + [y_peers[d - 1] for d in far_y] + around_peers
     for who in partners:
         pl.semaphore_signal(barrier, inc=1, device_id=who, device_id_type=MESH)
 
-    iota[...] = lax.broadcasted_iota(jnp.int32, iota.shape, 0).astype(jnp.int16)
-    for copy in loads:
-        copy.wait()
+    loads[0].wait()
+    loads[1].wait()
+    pl.semaphore_wait(barrier, len(partners))
 
     mid = n_z // 2
-    l = item_ix_ref[...]
-    grid_of = lax.shift_right_logical(l, per.bit_length() - 1)
-    l_z = lax.shift_right_logical(grid_of, 3)
-    l_x = lax.shift_right_logical(grid_of, 1) & 3
-    hi[...] = (grid_of & 1) * 2 + lax.shift_right_logical(l_x, 1)
-    l_slot = l_z + (mid - z)
-    l_slot = jnp.where(l_slot < 0, l_slot + n_z, jnp.where(l_slot >= n_z, l_slot - n_z, l_slot))
-    lo[...] = ((l_x & 1) * n_z + l_slot) * per + (l & (per - 1))
-    user_ref[...] = (user_ref[...] + (n_y - lax.rem(s + 2, n_y)) * u_dev) & (users - 1)
-    count_ref[...] = count_in[...].astype(F32)
-
-    pl.semaphore_wait(barrier, len(partners))
-
     pending = []
 
     def send(src, dst, send_sem, recv_sem, who):
@@ -170,14 +159,27 @@
             device_id=who, device_id_type=MESH,
         ).wait_recv()
 
-    by_reach = sorted(range(1, n_z), key=lambda d: -min(d, n_z - d))
     for d in by_reach:
         send(item_ref, table.at[c, x, (mid - d) % n_z], z_send.at[d - 1], z_recv.at[d - 1], z_peers[d - 1])
     table[c, x, mid] = item_ref[...]
-    far_y = sorted(range(1, n_y), key=lambda d: -min(d, n_y - d))
     for d in far_y:
         send(week_ref, weeks.at[s], w_send.at[d - 1], w_recv.at[d - 1], y_peers[d - 1])
     weeks[s] = week_ref[...]
+
+    iota[...] = lax.broadcasted_iota(jnp.int32, iota.shape, 0).astype(jnp.int16)
+    for copy in loads[2:]:
+        copy.wait()
+
+    l = item_ix_ref[...]
+    grid_of = lax.shift_right_logical(l, per.bit_length() - 1)
+    l_z = lax.shift_right_logical(grid_of, 3)
+    l_x = lax.shift_right_logical(grid_of, 1) & 3
+    hi[...] = ((grid_of & 1) ^ c) * 2 + lax.shift_right_logical(l_x, 1)
+    l_slot = l_z + (mid - z)
+    l_slot = jnp.where(l_slot < 0, l_slot + n_z, jnp.where(l_slot >= n_z, l_slot - n_z, l_slot))
+    lo[...] = ((l_x & 1) * n_z + l_slot) * per + (l & (per - 1))
+    user_ref[...] = (user_ref[...] + (n_y - lax.rem(s + 2, n_y)) * u_dev) & (users - 1)
+    count_ref[...] = count_in[...].astype(F32)
 
     def make_user(r, carry):
         col = pl.ds(pl.multiple_of(r * LANES, LANES), LANES)
@@ -269,71 +271,94 @@
     half = N_X * N_CORE // HI
 
     def turn(core):
-        sums = None
-        for j in range(HI // N_CORE):
-            part = table[core, j * half : (j + 1) * half].reshape(n_lo, rank)
-            columns = dot_nt(eye, part).astype(BF16)
-            tt[pl.ds(pl.multiple_of((core * (HI // N_CORE) + j) * rank, rank), rank), :] = columns
-            term = dot_nt(columns, columns)
-            sums = term if sums is None else sums + term
-        return sums
-
-    item_gram = turn(c)
+        rows = pl.ds(pl.multiple_of(core * own * rank, own * rank), own * rank)
+        tt[rows, :] = jnp.concatenate(
+            [
+                dot_nt(eye, table[core, j * half : (j + 1) * half].reshape(n_lo, rank)).astype(BF16)
+                for j in range(own)
+            ],
+            0,
+        )
+        return rows
+
+    own = HI // N_CORE
+    mine = turn(c)
+    own_gram = None
+    for j in range(own):
+        columns = tt[pl.ds(pl.multiple_of((c * own + j) * rank, rank), rank), :]
+        term = dot_nt(columns, columns)
+        own_gram = term if own_gram is None else own_gram + term
+    gram_part[...] = own_gram.reshape(gram_part.shape)
+    for d in far_y:
+        send(gram_part.at[x], gram_in.at[d - 1], g_send.at[d - 1], g_recv.at[d - 1], y_peers[d - 1])
+
+    per_blk = N_BLK // LANES
+    blocks = n_all // N_BLK
+
+    def look_up(rows, k, finish):
+        col = pl.ds(pl.multiple_of(k * N_BLK, N_BLK), N_BLK)
+        looked = jnp.dot(tt[rows, :], hot_item[:, col], preferred_element_type=F32)
+        parts = []
+        for q in range(per_blk):
+            part = looked[:, q * LANES : (q + 1) * LANES]
+            top = jnp.broadcast_to(hi[pl.ds(k * per_blk + q, 1), :], (rank, LANES))
+            parts.append(finish(k, q, top, part[:rank], part[rank:]))
+        kr_all[:, col] = jnp.concatenate(parts, 1)
+
+    def pick_own(k, carry):
+        look_up(mine, k, lambda k, q, top, low, high: jnp.where(top == 0, low, high).astype(BF16))
+        return carry
+
+    def finish_other(k, q, top, low, high):
+        at = pl.ds(pl.multiple_of(k * N_BLK + q * LANES, LANES), LANES)
+        value = jnp.where(top < 2, kr_all[:, at].astype(F32), jnp.where(top == 2, low, high))
+        return (value * scaled[:, at]).astype(BF16)
+
+    def add_users(k, span):
+        col = pl.ds(pl.multiple_of(k * N_BLK, N_BLK), N_BLK)
+        sums = dot_nt(hot_user[span.start * u_dev : span.stop * u_dev, col], kr_all[:, col])
+        total[span] += sums.reshape(span.stop - span.start, u_dev, rank)
+
+    def pick_other(k, carry):
+        look_up(other, k, finish_other)
+        add_users(k, slice(0, n_y))
+        return carry
+
+    total[...] = jnp.zeros_like(total)
+    lax.fori_loop(0, blocks, pick_own, 0)
+
     for d in range(N_X):
         spot = table.at[1 - c, x_at((N_X - d) % N_X)]
         arrived(spot, c_send.at[d], c_recv.at[d], c_peer)
-    item_gram = item_gram + turn(1 - c)
-    gram_part[...] = item_gram.reshape(gram_part.shape)
-    e = x * N_CORE + c
-    for d in far_y:
-        send(gram_part.at[e], gram_in.at[d - 1], g_send.at[d - 1], g_recv.at[d - 1], y_peers[d - 1])
-
-    per_blk = N_BLK // LANES
-
-    def main_block(k, carry):
-        col = pl.ds(pl.multiple_of(k * N_BLK, N_BLK), N_BLK)
-        looked = jnp.dot(tt[...], hot_item[:, col], preferred_element_type=F32)
-        kr = []
-        for q in range(per_blk):
-            top = jnp.broadcast_to(hi[pl.ds(k * per_blk + q, 1), :], (rank, LANES))
-            part = looked[:, q * LANES : (q + 1) * LANES]
-            value = part[(HI - 1) * rank :]
-            for j in range(HI - 2, -1, -1):
-                value = jnp.where(top == j, part[j * rank : (j + 1) * rank], value)
-            at = pl.ds(pl.multiple_of(k * N_BLK + q * LANES, LANES), LANES)
-            kr.append((value * scaled[:, at]).astype(BF16))
-        kr_all[:, col] = jnp.concatenate(kr, 1)
-        return carry
-
-    blocks = n_all // N_BLK
-    first = 3 * blocks // 4
-    lax.fori_loop(0, first, main_block, 0)
+    other = turn(1 - c)
+
+    lax.fori_loop(0, blocks // 2, pick_other, 0)
 
     for d in range(1, n_y):
         arrived(gram_in.at[d - 1], g_send.at[d - 1], g_recv.at[d - 1], y_peers[d - 1])
-    piece = gram_part[e]
+    piece = gram_part[x]
     for d in range(1, n_y):
         piece = piece + gram_in[d - 1]
-    gram_all[e] = piece
+    gram_all[c, x] = piece
     for k in range(len(around)):
-        send(gram_all.at[e], gram_all.at[e], h_send.at[k], h_recv.at[k], around_peers[k])
-
-    lax.fori_loop(first, blocks, main_block, 0)
-
-    half_users = users // 2
+        send(gram_all.at[c, x], gram_all.at[c, x], h_send.at[k], h_recv.at[k], around_peers[k])
+
+    lax.fori_loop(blocks // 2, blocks - 1, pick_other, 0)
+    look_up(other, blocks - 1, finish_other)
     for side in range(2):
-        span = slice(side * half_users, (side + 1) * half_users)
-        sums = dot_nt(hot_user[span, :], kr_all[...])
-        mine = range(side * n_y // 2, (side + 1) * n_y // 2)
-        total[side * n_y // 2 : (side + 1) * n_y // 2] = sums.reshape(n_y // 2, u_dev, rank)
+        held = range(side * n_y // 2, (side + 1) * n_y // 2)
+        add_users(blocks - 1, slice(held.start, held.stop))
         for d in far_y:
-            if (d - 2) % n_y in mine:
+            if (d - 2) % n_y in held:
                 send(total.at[(d - 2) % n_y], rows_in.at[d - 1], m_send.at[d - 1], m_recv.at[d - 1], y_peers[d - 1])
 
     for k, (dx, dc) in enumerate(around):
-        spot = gram_all.at[x_at((N_X - dx) % N_X) * N_CORE + core_at(dc)]
+        spot = gram_all.at[core_at(dc), x_at((N_X - dx) % N_X)]
         arrived(spot, h_send.at[k], h_recv.at[k], around_peers[k])
-    inverse = invert_spd(gram_all[...].reshape(rank, rank) * week_gram)
+    item_gram = gram_all[0]
+    for core in range(1, N_CORE):
+        item_gram = item_gram + gram_all[core]
+    inverse = invert_spd(item_gram.reshape(rank, rank) * week_gram)
 
     for d in range(1, n_y):
         arrived(rows_in.at[d - 1], m_send.at[d - 1], m_recv.at[d - 1], y_peers[d - 1])
@@ -388,16 +413,18 @@
             pltpu.VMEM((groups, LANES), jnp.int32),
             pltpu.VMEM((groups, LANES), jnp.int32),
             pltpu.VMEM((n_y, u_dev, rank), F32),
-            pltpu.VMEM((n_y, rank // n_y, rank), F32),
-            pltpu.VMEM((n_y - 1, rank // n_y, rank), F32),
-            pltpu.VMEM((n_y, rank // n_y, rank), F32),
+            pltpu.VMEM((N_X, rank // N_X, rank), F32),
+            pltpu.VMEM((n_y - 1, rank // N_X, rank), F32),
+            pltpu.VMEM((N_CORE, N_X, rank // N_X, rank), F32),
             pltpu.VMEM((n_y - 1, u_dev, rank), F32),
         ]
         + [dma((6,))]
         + [dma((n_z - 1,))] * 2
         + [dma((N_X - 1,))] * 2
         + [dma((N_X,))] * 2
-        + [dma((n_y - 1,))] * 8,
+        + [dma((n_y - 1,))] * 4
+        + [dma((N_X * N_CORE - 1,))] * 2
+        + [dma((n_y - 1,))] * 2,
         compiler_params=pltpu.CompilerParams(
             collective_id=0, has_side_effects=True, vmem_limit_bytes=62914560
         ),

time: 56.4 us -> 54.1 us (0.959)
  Pallas kernels: 54.7 us -> 52.5 us
    pallas_call x1, Pallas kernels: 54.7 us -> 52.5 us  [local(): pl.pallas_call(functools.partial(kernel, n_z, n_y), out_shape=jax.ShapeDt...]
where the time goes in v3:
time: 54.1 us; the launch traced here: 53.9 us
  Pallas kernels  52.5 us (97%)
  local copies, waits for them, and re-layouts  1.38 us (3%)
    pallas_call x1, Pallas kernels, local(): pl.pallas_call(functools.partial(kernel, n_z, n_y), out_shape=jax.ShapeDt...  52.5 us
    unnamed x1, local copies, waits for them, and re-layouts  1.38 us

profile of v3, /device:TPU:1, one launch (start us, length us, event | category | flops | bytes accessed | tf_op | source)
XLA Modules:
  0.0 53.9 jit_solution(4532629933707747452)
XLA Ops:
  0.0 52.5 %mttkrp_solve.1 = f32[64,128]{1,0:T(8,128)} custom-call(s32[64,128]{1,0:T(8,128)} %bitcast.4, s32[64,128]{1,0:T(8,128)} %bitcast.5, s32[64,128]{1,0:T(8,128)} %bitcast.6, bf16[64,128]{1,0:T(8,128)(2,1)} %bitcast.7, bf16[32,128]{1,0:T(8,128)(2,1)} %item_hbm.1, bf16[64,128]{1,0:T(8,128)(2,1)} %week_hbm.1), custom_call_target="tpu_custom_call" | custom-call | tf_op jit(solution)/shard_map/mttkrp_solve/pallas_call | solution.py:391
  52.5 1.4 %copy.8 = f32[64,128]{1,0:T(8,128)} copy(f32[64,128]{1,0:T(8,128)} %mttkrp_solve.1) | data formatting | bytes 65536

commit v4 on v3

--- a/solution.py
+++ b/solution.py
@@ -160,8 +160,8 @@
         ).wait_recv()
 
     for d in by_reach:
-        send(item_ref, table.at[c, x, (mid - d) % n_z], z_send.at[d - 1], z_recv.at[d - 1], z_peers[d - 1])
-    table[c, x, mid] = item_ref[...]
+        send(item_ref, table.at[c, 0, (mid - d) % n_z], z_send.at[d - 1], z_recv.at[d - 1], z_peers[d - 1])
+    table[c, 0, mid] = item_ref[...]
     for d in far_y:
         send(week_ref, weeks.at[s], w_send.at[d - 1], w_recv.at[d - 1], y_peers[d - 1])
     weeks[s] = week_ref[...]
@@ -173,7 +173,7 @@
     l = item_ix_ref[...]
     grid_of = lax.shift_right_logical(l, per.bit_length() - 1)
     l_z = lax.shift_right_logical(grid_of, 3)
-    l_x = lax.shift_right_logical(grid_of, 1) & 3
+    l_x = (lax.shift_right_logical(grid_of, 1) + (N_X - x)) & 3
     hi[...] = ((grid_of & 1) ^ c) * 2 + lax.shift_right_logical(l_x, 1)
     l_slot = l_z + (mid - z)
     l_slot = jnp.where(l_slot < 0, l_slot + n_z, jnp.where(l_slot >= n_z, l_slot - n_z, l_slot))
@@ -196,13 +196,13 @@
     def z_arrive(lo_reach, hi_reach):
         for reach in range(lo_reach, hi_reach + 1):
             for d in sorted({reach, n_z - reach}):
-                arrived(table.at[c, x, (mid - d) % n_z], z_send.at[d - 1], z_recv.at[d - 1], z_peers[d - 1])
+                arrived(table.at[c, 0, (mid - d) % n_z], z_send.at[d - 1], z_recv.at[d - 1], z_peers[d - 1])
 
     def pass_on(first, count):
-        part = table.at[c, x, pl.ds(first, count)]
+        part = table.at[c, 0, pl.ds(first, count)]
         for d in far_x:
             copy = pltpu.make_async_remote_copy(
-                src_ref=part, dst_ref=part, send_sem=x_send.at[d - 1], recv_sem=x_recv.at[d - 1],
+                src_ref=part, dst_ref=table.at[c, N_X - d, pl.ds(first, count)], send_sem=x_send.at[d - 1], recv_sem=x_recv.at[d - 1],
                 device_id=x_peers[d - 1], device_id_type=MESH,
             )
             copy.start()
@@ -222,7 +222,7 @@
     pass_on(0, mid - wide)
     if n_z - (mid + wide + 1):
         pass_on(mid + wide + 1, n_z - (mid + wide + 1))
-    send(table.at[c, x], table.at[c, x], c_send.at[0], c_recv.at[0], c_peer)
+    send(table.at[c, 0], table.at[c, 0], c_send.at[0], c_recv.at[0], c_peer)
 
     eye = jnp.where(
         lax.broadcasted_iota(jnp.int32, (rank, rank), 0)
@@ -263,26 +263,67 @@
 
     lax.fori_loop(0, n_all // WEEK_BLK, week_block, 0)
 
-    for d in range(1, N_X):
-        spot = table.at[c, x_at(N_X - d)]
+    def x_arrive(d):
+        spot = table.at[c, N_X - d]
         arrived(spot, x_send.at[d - 1], x_recv.at[d - 1], x_peers[d - 1])
         send(spot, spot, c_send.at[d], c_recv.at[d], c_peer)
 
     half = N_X * N_CORE // HI
 
-    def turn(core):
-        rows = pl.ds(pl.multiple_of(core * own * rank, own * rank), own * rank)
-        tt[rows, :] = jnp.concatenate(
-            [
-                dot_nt(eye, table[core, j * half : (j + 1) * half].reshape(n_lo, rank)).astype(BF16)
-                for j in range(own)
-            ],
-            0,
-        )
+    own = HI // N_CORE
+
+    def turn(core, j):
+        rows = pl.ds(pl.multiple_of((core * own + j) * rank, rank), rank)
+        tt[rows, :] = dot_nt(eye, table[core, j * half : (j + 1) * half].reshape(n_lo, rank)).astype(BF16)
         return rows
 
-    own = HI // N_CORE
-    mine = turn(c)
+    per_blk = N_BLK // LANES
+    blocks = n_all // N_BLK
+
+    def look_up(rows, k, finish):
+        col = pl.ds(pl.multiple_of(k * N_BLK, N_BLK), N_BLK)
+        looked = jnp.dot(tt[rows, :], hot_item[:, col], preferred_element_type=F32)
+        parts = []
+        for q in range(per_blk):
+            part = looked[:, q * LANES : (q + 1) * LANES]
+            top = jnp.broadcast_to(hi[pl.ds(k * per_blk + q, 1), :], (rank, LANES))
+            parts.append(finish(k, q, top, part[:rank], part[-rank:]))
+        kr_all[:, col] = jnp.concatenate(parts, 1)
+
+    def pick_first(k, carry):
+        look_up(first_rows, k, lambda k, q, top, low, high: low.astype(BF16))
+        return carry
+
+    def finish_second(k, q, top, low, high):
+        at = pl.ds(pl.multiple_of(k * N_BLK + q * LANES, LANES), LANES)
+        return jnp.where(top == 0, kr_all[:, at].astype(F32), low).astype(BF16)
+
+    def pick_second(k, carry):
+        look_up(second_rows, k, finish_second)
+        return carry
+
+    def finish_other(k, q, top, low, high):
+        at = pl.ds(pl.multiple_of(k * N_BLK + q * LANES, LANES), LANES)
+        value = jnp.where(top < 2, kr_all[:, at].astype(F32), jnp.where(top == 2, low, high))
+        return (value * scaled[:, at]).astype(BF16)
+
+    def add_users(k, span):
+        col = pl.ds(pl.multiple_of(k * N_BLK, N_BLK), N_BLK)
+        sums = dot_nt(hot_user[span.start * u_dev : span.stop * u_dev, col], kr_all[:, col])
+        total[span] += sums.reshape(span.stop - span.start, u_dev, rank)
+
+    def pick_other(k, carry):
+        look_up(other, k, finish_other)
+        add_users(k, slice(0, n_y))
+        return carry
+
+    total[...] = jnp.zeros_like(total)
+    x_arrive(N_X - 1)
+    first_rows = turn(c, 0)
+    lax.fori_loop(0, blocks, pick_first, 0)
+    for d in range(1, N_X - 1):
+        x_arrive(d)
+    second_rows = turn(c, 1)
     own_gram = None
     for j in range(own):
         columns = tt[pl.ds(pl.multiple_of((c * own + j) * rank, rank), rank), :]
@@ -292,45 +333,14 @@
     for d in far_y:
         send(gram_part.at[x], gram_in.at[d - 1], g_send.at[d - 1], g_recv.at[d - 1], y_peers[d - 1])
 
-    per_blk = N_BLK // LANES
-    blocks = n_all // N_BLK
-
-    def look_up(rows, k, finish):
-        col = pl.ds(pl.multiple_of(k * N_BLK, N_BLK), N_BLK)
-        looked = jnp.dot(tt[rows, :], hot_item[:, col], preferred_element_type=F32)
-        parts = []
-        for q in range(per_blk):
-            part = looked[:, q * LANES : (q + 1) * LANES]
-            top = jnp.broadcast_to(hi[pl.ds(k * per_blk + q, 1), :], (rank, LANES))
-            parts.append(finish(k, q, top, part[:rank], part[rank:]))
-        kr_all[:, col] = jnp.concatenate(parts, 1)
-
-    def pick_own(k, carry):
-        look_up(mine, k, lambda k, q, top, low, high: jnp.where(top == 0, low, high).astype(BF16))
-        return carry
-
-    def finish_other(k, q, top, low, high):
-        at = pl.ds(pl.multiple_of(k * N_BLK + q * LANES, LANES), LANES)
-        value = jnp.where(top < 2, kr_all[:, at].astype(F32), jnp.where(top == 2, low, high))
-        return (value * scaled[:, at]).astype(BF16)
-
-    def add_users(k, span):
-        col = pl.ds(pl.multiple_of(k * N_BLK, N_BLK), N_BLK)
-        sums = dot_nt(hot_user[span.start * u_dev : span.stop * u_dev, col], kr_all[:, col])
-        total[span] += sums.reshape(span.stop - span.start, u_dev, rank)
-
-    def pick_other(k, carry):
-        look_up(other, k, finish_other)
-        add_users(k, slice(0, n_y))
-        return carry
-
-    total[...] = jnp.zeros_like(total)
-    lax.fori_loop(0, blocks, pick_own, 0)
+    lax.fori_loop(0, blocks, pick_second, 0)
 
     for d in range(N_X):
-        spot = table.at[1 - c, x_at((N_X - d) % N_X)]
+        spot = table.at[1 - c, (N_X - d) % N_X]
         arrived(spot, c_send.at[d], c_recv.at[d], c_peer)
-    other = turn(1 - c)
+    for j in range(own):
+        turn(1 - c, j)
+    other = pl.ds(pl.multiple_of((1 - c) * own * rank, own * rank), own * rank)
 
     lax.fori_loop(0, blocks // 2, pick_other, 0)
 
@@ -370,7 +380,7 @@
     for copy in pending:
         copy.wait_send()
     for d in range(1, N_X):
-        slab = table.at[c, x]
+        slab = table.at[c, 0]
         pltpu.make_async_remote_copy(
             src_ref=slab, dst_ref=slab, send_sem=x_send.at[d - 1], recv_sem=x_recv.at[d - 1],
             device_id=x_peers[d - 1], device_id_type=MESH,

time: 54.1 us -> 55.6 us (1.028)
  Pallas kernels: 52.5 us -> 54 us
    pallas_call x1, Pallas kernels: 52.5 us -> 54 us  [local(): pl.pallas_call(functools.partial(kernel, n_z, n_y), out_shape=jax.ShapeDt...]
where the time goes in v4:
time: 55.6 us; the launch traced here: 55.4 us
  Pallas kernels  54 us (97%)
  local copies, waits for them, and re-layouts  1.38 us (2%)
    pallas_call x1, Pallas kernels, local(): pl.pallas_call(functools.partial(kernel, n_z, n_y), out_shape=jax.ShapeDt...  54 us
    unnamed x1, local copies, waits for them, and re-layouts  1.38 us

profile of v4, /device:TPU:1, one launch (start us, length us, event | category | flops | bytes accessed | tf_op | source)
XLA Modules:
  0.0 55.4 jit_solution(4878501533475441541)
XLA Ops:
  0.0 54.0 %mttkrp_solve.1 = f32[64,128]{1,0:T(8,128)} custom-call(s32[64,128]{1,0:T(8,128)} %bitcast.4, s32[64,128]{1,0:T(8,128)} %bitcast.5, s32[64,128]{1,0:T(8,128)} %bitcast.6, bf16[64,128]{1,0:T(8,128)(2,1)} %bitcast.7, bf16[32,128]{1,0:T(8,128)(2,1)} %item_hbm.1, bf16[64,128]{1,0:T(8,128)(2,1)} %week_hbm.1), custom_call_target="tpu_custom_call" | custom-call | tf_op jit(solution)/shard_map/mttkrp_solve/pallas_call | solution.py:401
  54.0 1.4 %copy.8 = f32[64,128]{1,0:T(8,128)} copy(f32[64,128]{1,0:T(8,128)} %mttkrp_solve.1) | data formatting | bytes 65536
